TPU v7x, 256 devices: a whole 4x4x8 slice. The times are simulated.
256 devices in a mesh: section: 4 (over z_lo, core), dp: 4 (over y), vocab: 16 (over z_hi, x).
Axes of the slice: x: 4, y: 4, z: 8 (z_hi: 4, z_lo: 2; z = z_hi * 2 + z_lo), core: 2. Of those that a mesh axis runs over, the one named last changes fastest.
Arguments:
- hidden: bfloat16 [1024, 5120], P('dp', ('section', 'vocab')), may hold values from -1.5 to 1.5
- norm_gain: bfloat16 [5120], P(('section', 'vocab')), may hold values from 0.5 to 1.5
- head: bfloat16 [5120, 151936], P('dp', ('section', 'vocab')), may hold values from -0.25 to 0.25
- token_ids: int32 [1024], P('dp'), may hold values from 0 to 151935
- entropy_mask: int32 [1024], P('dp'), may hold values 0 or 1
- group_ids: int32 [1024], P('dp'), may hold values from 0 to 31, as said below
- old_logp: float32 [1024], P('dp'), may hold values from -30 to 0
- scores: float32 [1024], P('dp'), may hold values from -6 to 6
Outputs:
- new_logp: float32 [1024], P('dp')
- entropy: float32 [1024], P('dp')
- grad_hidden: bfloat16 [1024, 5120], P('dp', ('section', 'vocab'))
Inputs may be any that keep to these rules, and one draw needn't show every extreme that they name: `group_ids`: tokens of the i-th block of 256 rows carry group ids from i * 8 to (i + 1) * 8 - 1, each of these at least once.
All inputs are finite; a program needn't handle non-finite values. No bound on the sum of `entropy_mask` on one device may be relied on, other than what follows from the above.
Results may differ from a plain program's by a relative error of at most 0.0095.
Values may be sent and summed in bfloat16 or wider, within the bound.
No kernel may reach another device: no remote copies, remote signals or barrier semaphores. Data moves between devices by JAX's collectives and lax.ppermute only.
A program may use at most 128 MiB of HBM per device.

v0:
```python
import functools

import jax
import jax.numpy as jnp
from jax import lax
from jax.experimental import pallas as pl
from jax.experimental.pallas import tpu as pltpu
from jax.sharding import PartitionSpec as P

NORM_EPSILON = 1e-06
LOW_CLIP = 0.5
HIGH_CLIP = 2.0
GPD = 8
CHUNK = 64
SHARE = 80
TILE = 400
EXTRA = 16
HALF_TILES = 3
BIG = 32000.0
REL = (3, 1, 2, 0)
SECTION, DP, VOCAB = "section", "dp", "vocab"
f32, bf16, i16, i32 = jnp.float32, jnp.bfloat16, jnp.int16, jnp.int32
CORE_SWAP = ((0, 1), (1, 0), (2, 3), (3, 2))
UP = tuple((i, (i + 1) % 4) for i in range(4))
DOWN = tuple((i, (i + 3) % 4) for i in range(4))
X_GROUPS = [[z * 4 + x for x in range(4)] for z in range(4)]
Z_GROUPS = [[(a * 2 + c) * 16 + b * 4 + x for a in range(2) for b in range(4)] for c in range(2) for x in range(4)]
STEP = tuple((s * 4 + d, s * 4 + (d + (3 if s % 2 else 1)) % 4) for s in range(4) for d in range(4))
CORE_GROUPS = [[(z * 2 + c) * 16 + v for z in range(2) for v in range(16)] for c in range(2)]
SPREAD = tuple((d * 4 + (d + REL[s]) % 4, s * 4 + d) for s in range(4) for d in range(4))
COLLECT = tuple((b, a) for a, b in SPREAD)
SMALL = pltpu.CompilerParams(vmem_limit_bytes=10 * 1024 * 1024)
LARGE = pltpu.CompilerParams(vmem_limit_bytes=20 * 1024 * 1024)


def decode(block):
    codes = block[:TILE].astype(f32)
    power = block[TILE : TILE + EXTRA].astype(f32)[:1]
    return codes * (jnp.exp2(power - 15.0) * (32768.0 / BIG))


def encode(part, square_sum, out_ref, tile):
    start = tile * (TILE + EXTRA)
    top = jnp.max(jnp.abs(part), axis=0, keepdims=True)
    power = jnp.clip(jnp.floor(jnp.log2(jnp.maximum(top, 1e-30))) + 1.0, -90.0, 90.0)
    codes = part * (jnp.exp2(15.0 - power) * (BIG / 32768.0))
    codes = jnp.clip(jnp.round(codes), -32767.0, 32767.0)
    sum_power = jnp.clip(jnp.floor(jnp.log2(jnp.maximum(square_sum, 1e-30))) + 1.0, -100.0, 100.0)
    scaled = square_sum * jnp.exp2(15.0 - sum_power)
    high = jnp.minimum(jnp.floor(scaled), 32767.0)
    spare = jnp.zeros((EXTRA - 4, part.shape[1]), f32)
    extra = jnp.concatenate([power, sum_power, high, jnp.round((scaled - high) * 16384.0), spare], axis=0)
    out_ref[start : start + TILE] = codes.astype(i32).astype(i16)
    out_ref[start + TILE : start + TILE + EXTRA] = extra.astype(i32).astype(i16)


def decode_sum(block):
    extra = block[TILE : TILE + EXTRA].astype(f32)
    return (extra[2:3] + extra[3:4] * (1.0 / 16384.0)) * jnp.exp2(extra[1:2] - 15.0)


def inside(part, rows, start):
    index = lax.broadcasted_iota(i32, part.shape, 0) + start
    return jnp.where(index < rows, part, 0.0)


def first_kernel(rows, half, head_ref, x_ref, sum_ref, out_ref):
    for tile in range(HALF_TILES):
        at = tile * TILE
        part = jnp.dot(head_ref[at : at + TILE], x_ref[...], preferred_element_type=f32)
        if (half * HALF_TILES + tile + 1) * TILE > rows:
            part = inside(part, rows, (half * HALF_TILES + tile) * TILE)
        encode(part, sum_ref[...], out_ref, tile)


def first_message(head_t, x, square_sum, half):
    rows, feats = head_t.shape
    tokens = x.shape[1]
    block = TILE + EXTRA
    whole = lambda i: (0, 0)
    return pl.pallas_call(
        functools.partial(first_kernel, rows, half),
        out_shape=jax.ShapeDtypeStruct((HALF_TILES * block, tokens), i16),
        grid=(1,),
        in_specs=[
            pl.BlockSpec((HALF_TILES * TILE, feats), lambda i: (half, 0)),
            pl.BlockSpec((feats, tokens), whole),
            pl.BlockSpec((1, tokens), whole),
        ],
        out_specs=pl.BlockSpec((HALF_TILES * block, tokens), whole),
        compiler_params=SMALL,
        cost_estimate=pl.CostEstimate(
            flops=rows * feats * tokens, bytes_accessed=4 * rows * feats, transcendentals=0
        ),
    )(head_t, x, square_sum)


def message_kernel(half, part_ref, sum_ref, arrived_ref, out_ref):
    block = TILE + EXTRA
    for tile in range(HALF_TILES):
        at = (half * HALF_TILES + tile) * TILE
        arrived = arrived_ref[tile * block : (tile + 1) * block]
        encode(part_ref[at : at + TILE] + decode(arrived), sum_ref[...] + decode_sum(arrived), out_ref, tile)


def message(part, square_sum, half, arrived):
    return pl.pallas_call(
        functools.partial(message_kernel, half),
        out_shape=jax.ShapeDtypeStruct(arrived.shape, i16),
        compiler_params=SMALL,
        cost_estimate=pl.CostEstimate(
            flops=8 * arrived.size, bytes_accessed=8 * arrived.size, transcendentals=0
        ),
    )(part, square_sum, arrived)


def base_kernel(rows, head_ref, x_ref, out_ref):
    part = jnp.dot(head_ref[...], x_ref[...], preferred_element_type=f32)
    out_ref[...] = inside(part, rows, pl.program_id(0) * HALF_TILES * TILE)


def base(head_t, x):
    rows, feats = head_t.shape
    tokens = x.shape[1]
    return pl.pallas_call(
        functools.partial(base_kernel, rows),
        out_shape=jax.ShapeDtypeStruct((2 * HALF_TILES * TILE, tokens), f32),
        grid=(2,),
        in_specs=[
            pl.BlockSpec((HALF_TILES * TILE, feats), lambda i: (i, 0)),
            pl.BlockSpec((feats, tokens), lambda i: (0, 0)),
        ],
        out_specs=pl.BlockSpec((HALF_TILES * TILE, tokens), lambda i: (i, 0)),
        compiler_params=LARGE,
        cost_estimate=pl.CostEstimate(
            flops=2 * rows * feats * tokens, bytes_accessed=2 * rows * feats, transcendentals=0
        ),
    )(head_t, x)


def finish_kernel(rows, feats, base_ref, a_ref, b_ref, sum_ref, target_ref, pick_ref, e_ref, mine_ref, stats_ref, logits, exps):
    tokens = base_ref.shape[1]
    block = TILE + EXTRA
    square_sum = sum_ref[...] + decode_sum(a_ref[:block, :])
    inverse = lax.rsqrt(square_sum / feats + NORM_EPSILON)
    top = jnp.full((1, tokens), -1e30, f32)
    for tile in range(2 * HALF_TILES):
        at = tile * TILE
        ref, place = (a_ref, tile) if tile < HALF_TILES else (b_ref, tile - HALF_TILES)
        value = (base_ref[at : at + TILE, :] + decode(ref[place * block : (place + 1) * block, :])) * inverse
        if at + TILE > rows:
            index = lax.broadcasted_iota(i32, value.shape, 0) + at
            value = jnp.where(index < rows, value, -1e30)
        logits[at : at + TILE, :] = value
        top = jnp.maximum(top, jnp.max(value, axis=0, keepdims=True))
    total = jnp.zeros((1, tokens), f32)
    weighted = jnp.zeros((1, tokens), f32)
    target = jnp.zeros((1, tokens), f32)
    place = lax.broadcasted_iota(i32, (TILE, tokens), 0)
    for tile in range(2 * HALF_TILES):
        at = tile * TILE
        value = logits[at : at + TILE, :]
        e = jnp.exp(value - top)
        total += jnp.sum(e, axis=0, keepdims=True)
        weighted += jnp.sum(e * value, axis=0, keepdims=True)
        target += jnp.sum(jnp.where(place == target_ref[...] - at, value, 0.0), axis=0, keepdims=True)
        exps[at : at + TILE, :] = e.astype(bf16)
    spare = exps.shape[0] - 2 * HALF_TILES * TILE
    exps[2 * HALF_TILES * TILE :, :] = jnp.zeros((spare, tokens), bf16)
    stats_ref[...] = jnp.concatenate([top, total, weighted, target, inverse], axis=0)
    mine = lax.dot_general(pick_ref[...], exps[...], (((1,), (1,)), ((), ())), preferred_element_type=f32)
    mine_ref[...] = mine[:, :rows].astype(bf16)
    e_ref[...] = exps[:rows, :]


def finish(rows, feats, total, a, b, square_sum, target, pick):
    tokens = total.shape[1]
    padded = -(-rows // 128) * 128
    return pl.pallas_call(
        functools.partial(finish_kernel, rows, float(feats)),
        out_shape=(
            jax.ShapeDtypeStruct((rows, tokens), bf16),
            jax.ShapeDtypeStruct((CHUNK, rows), bf16),
            jax.ShapeDtypeStruct((5, tokens), f32),
        ),
        scratch_shapes=[pltpu.VMEM((2 * HALF_TILES * TILE, tokens), f32), pltpu.VMEM((padded, tokens), bf16)],
        compiler_params=LARGE,
        cost_estimate=pl.CostEstimate(
            flops=2 * rows * CHUNK * tokens, bytes_accessed=10 * rows * tokens, transcendentals=rows * tokens
        ),
    )(total, a, b, square_sum, target, pick)


def grad_kernel(rows, core_ref, r0, r1, r2, r3, factor_ref, head_ref, keep_ref, give_ref, left, prod):
    @pl.when(pl.program_id(0) == 0)
    def _():
        for t, ref in enumerate((r0, r1, r2, r3)):
            @pl.loop(0, CHUNK // 16)
            def _(step, t=t, ref=ref):
                here = pl.ds(pl.multiple_of(step * 16, 16), 16)
                factor = factor_ref[pl.ds(pl.multiple_of(t * CHUNK + step * 16, 16), 16), :]
                index = lax.broadcasted_iota(i32, (16, rows), 1)
                hard = jnp.where(index == factor[:, 2:3].astype(i32), factor[:, 1:2], 0.0)
                value = ref[here, :].astype(f32) * factor[:, 0:1] + hard
                left[pl.ds(pl.multiple_of(t * CHUNK + step * 16, 16), 16), :] = value.astype(bf16)

    out = jnp.dot(left[...], head_ref[...], preferred_element_type=f32)
    for t in range(4):
        prod[t * 128 : t * 128 + CHUNK, :] = out[t * CHUNK : (t + 1) * CHUNK]
    core = core_ref[0]
    tile = head_ref.shape[1]
    for z in range(2):
        for ref, side in ((keep_ref, core), (give_ref, 1 - core)):
            at = pl.multiple_of((z * 2 + side) * 128, 128)
            turned = prod[pl.ds(at, 128), :].T
            lane = lax.broadcasted_iota(i32, (SHARE // 2, 128), 1)
            for group in range(tile // SHARE):
                top = turned[group * SHARE : group * SHARE + SHARE // 2]
                low = turned[group * SHARE + SHARE // 2 : (group + 1) * SHARE]
                packed = jnp.where(lane < CHUNK, top, pltpu.roll(low, CHUNK, 1))
                ref[z, group * SHARE // 2 : (group + 1) * SHARE // 2] = packed.astype(bf16)


def grad_product(head_t, rows, factors, core):
    cols, feats = head_t.shape
    tile = 640
    out = jax.ShapeDtypeStruct((2, feats // 2, 128), bf16)
    out_spec = pl.BlockSpec((2, tile // 2, 128), lambda i, c: (0, i, 0))
    return pl.pallas_call(
        functools.partial(grad_kernel, cols),
        out_shape=(out, out),
        grid_spec=pltpu.PrefetchScalarGridSpec(
            num_scalar_prefetch=1,
            grid=(feats // tile,),
            in_specs=[
                *[pl.BlockSpec((CHUNK, cols), lambda i, c: (0, 0)) for r in rows],
                pl.BlockSpec((4 * CHUNK, factors.shape[1]), lambda i, c: (0, 0)),
                pl.BlockSpec((cols, tile), lambda i, c: (0, i)),
            ],
            out_specs=(out_spec, out_spec),
            scratch_shapes=[pltpu.VMEM((4 * CHUNK, cols), bf16), pltpu.VMEM((512, tile), f32)],
        ),
        compiler_params=LARGE,
        cost_estimate=pl.CostEstimate(
            flops=8 * CHUNK * cols * feats, bytes_accessed=4 * cols * feats, transcendentals=0
        ),
    )(core.reshape(1), *rows, factors, head_t)


def share(value, axes, count, groups=None):
    copies = jnp.broadcast_to(value[None], (count, *value.shape))
    return lax.all_to_all(copies, axes, 0, 0, tiled=True, axis_index_groups=groups)


def shards(hidden, norm_gain, head, token_ids, entropy_mask, group_ids, old_logp, scores):
    tokens, share_cols = hidden.shape
    feats, vocab_cols = head.shape
    section, dp = lax.axis_index(SECTION), lax.axis_index(DP)
    core, low = section % 2, section // 2
    slice_index = lax.axis_index((SECTION, VOCAB))
    head_t = head.T
    hidden_t = hidden.T.astype(f32)
    gain = norm_gain.astype(f32)[:, None]

    rest = jnp.sum(hidden_t * hidden_t, axis=0, keepdims=True)
    pieces = []
    for _ in range(3):
        pieces.append(lax.reduce_precision(rest, 8, 7))
        rest = rest - pieces[-1]
    own = jnp.concatenate([hidden_t * gain, *pieces, jnp.zeros((5, tokens), f32)]).astype(bf16)
    own = lax.ppermute(own, (SECTION, DP), SPREAD)
    lines = share(own, (SECTION, VOCAB), 8, Z_GROUPS)

    blocks = share(lines, VOCAB, 4, X_GROUPS).reshape(4, 2, 4, share_cols + 8, tokens)
    sums = jnp.sum(blocks[:, :, :, share_cols:].astype(f32), axis=(0, 2, 3))
    blocks = blocks[:, :, :, :share_cols].transpose(1, 2, 0, 3, 4).reshape(2, feats, tokens)

    def send(part):
        return lax.ppermute(part, (SECTION, DP), STEP)

    first, later = blocks[0], blocks[1]
    p1 = send(first_message(head_t, first, sums[:1], 0))
    q1 = send(first_message(head_t, first, sums[:1], 1))
    later_pair = lax.ppermute(later, SECTION, CORE_SWAP)
    first_pair = lax.ppermute(first, SECTION, CORE_SWAP)
    sums, later_pair = lax.optimization_barrier((sums, later_pair))
    sums_pair = lax.ppermute(sums, SECTION, CORE_SWAP)
    is_even = core == 0
    second_sum, last_sum = jnp.where(is_even, sums, sums_pair)[1:], jnp.where(is_even, sums_pair, sums)[1:]
    second, last = jnp.where(is_even, later, later_pair), jnp.where(is_even, later_pair, later)
    part2, part3 = lax.optimization_barrier((base(head_t, second), base(head_t, first_pair)))
    p2 = send(message(part2, second_sum, 0, p1))
    q2 = send(message(part2, second_sum, 1, q1))
    p3 = send(message(part3, sums_pair[:1], 0, p2))
    q3 = message(part3, sums_pair[:1], 1, q2)
    q3 = send(q3)
    local_target = token_ids - slice_index * vocab_cols
    local_target = jnp.where(local_target < vocab_cols, local_target, -1)

    chosen = entropy_mask != 0
    position = jnp.where(chosen, jnp.cumsum(chosen.astype(i32)) - 1, -1)
    count = jnp.sum(chosen.astype(i32))
    slots = jnp.arange(CHUNK, dtype=i32)
    pick0 = position[None, :] == slots[:, None]

    own_part = base(head_t, last)
    exps, mine0, stats = finish(
        vocab_cols, share_cols * 64, own_part, p3, q3, last_sum, local_target[None], pick0.astype(bf16)
    )

    def send_rows(mine):
        from_below = lax.ppermute(mine, DP, UP)
        from_above = lax.ppermute(mine, DP, DOWN)
        return from_above, from_below, mine

    def gather_rows(chunk):
        pick = position[None, :] == (slots + chunk * CHUNK)[:, None]
        mine = lax.dot_general(
            pick.astype(bf16), exps, (((1,), (1,)), ((), ())), preferred_element_type=f32
        ).astype(bf16)
        return pick, send_rows(mine)

    rows0 = send_rows(mine0)

    inverse = stats[4]
    every = share(stats[:4], (SECTION, VOCAB), 64)
    row_top = jnp.max(every[:, 0], axis=0)
    scale = jnp.exp(every[:, 0] - row_top)
    exp_total = jnp.sum(scale * every[:, 1], axis=0)
    weighted = jnp.sum(scale * every[:, 2], axis=0)
    target = jnp.sum(every[:, 3], axis=0)
    log_total = row_top + jnp.log(exp_total)
    mean_logit = weighted / exp_total
    entropy = log_total - mean_logit
    new_logp = target - log_total
    first_group = dp * GPD
    members = (
        group_ids[:, None] == first_group + jnp.arange(GPD, dtype=i32)[None, :]
    ).astype(f32)
    group_sum = jnp.sum(scores[:, None] * members, axis=0)
    group_count = jnp.sum(members, axis=0)
    advantage = scores - jnp.sum(members * (group_sum / group_count)[None], axis=1)
    weight = jnp.clip(jnp.exp(new_logp - old_logp), LOW_CLIP, HIGH_CLIP)
    grad_logp = -entropy_mask.astype(f32) * weight * advantage
    soft = -grad_logp * jnp.exp(stats[0] - row_top) / exp_total

    def chunk_grad(pick, rows):
        values = jnp.stack([soft, grad_logp, token_ids.astype(f32), jnp.broadcast_to(count.astype(f32), soft.shape)])
        picked = jnp.sum(jnp.where(pick[None], values[:, None, :], 0.0), axis=2)
        picked = picked.at[3].set(count.astype(f32))
        from_above, from_below, mine = rows
        picked, from_above, from_below = lax.optimization_barrier((picked, from_above, from_below))
        across = lax.ppermute(jnp.where(core == 0, from_below, from_above), (SECTION, DP), STEP)
        rows = from_below, from_above, across, mine
        factors = share(picked, DP, 4)
        most = jnp.max(factors[:, 3, 0]).astype(i32)
        factors = jnp.stack([lax.dynamic_index_in_dim(factors, (dp + r) % 4, 0, False) for r in REL])
        factors = factors.transpose(0, 2, 1).reshape(4 * CHUNK, 4)
        factors = factors - jnp.array([0, 0, 1, 0], f32) * (slice_index * vocab_cols).astype(f32)

        keep, give = grad_product(head_t, rows, factors, core)
        part = (keep.astype(f32) + lax.ppermute(give, SECTION, CORE_SWAP).astype(f32)).astype(bf16)
        part = part.reshape(32, -1, part.shape[-1])
        part = lax.all_to_all(
            part, (SECTION, VOCAB), 0, 0, tiled=True, axis_index_groups=CORE_GROUPS
        )
        part = jnp.sum(part.astype(f32), axis=0)
        part = jnp.concatenate([part[:, :CHUNK], part[:, CHUNK:]], axis=0)
        part = lax.ppermute(part, (SECTION, DP), COLLECT)
        return jnp.dot(part, pick.astype(f32), precision=lax.Precision.HIGHEST), most

    grad, most = chunk_grad(pick0, rows0)

    def more(state):
        chunk, total = state
        part, _ = chunk_grad(*gather_rows(chunk))
        return chunk + 1, total + part

    _, grad = lax.while_loop(lambda state: state[0] * CHUNK < most, more, (jnp.ones((), i32), grad))

    inner = grad_logp * (target - mean_logit) / (share_cols * 64)
    unit = hidden_t * inverse
    grad_hidden = inverse * (gain * grad - unit * inner[None])
    return new_logp, entropy, grad_hidden.astype(bf16).T


def solution(mesh):
    in_specs = (
        P("dp", ("section", "vocab")),
        P(("section", "vocab")),
        P("dp", ("section", "vocab")),
        P("dp"),
        P("dp"),
        P("dp"),
        P("dp"),
        P("dp"),
    )
    out_specs = (P("dp"), P("dp"), P("dp", ("section", "vocab")))
    return jax.shard_map(shards, mesh=mesh, in_specs=in_specs, out_specs=out_specs, check_vma=False)
```

profile of v0, /device:TPU:16, one launch (start us, length us, event | category | flops | bytes accessed | tf_op | source)
XLA Modules:
  0.0 179.0 jit_solution(18407197375132273193)
XLA Ops:
  2.2 3.6 %collective-permute-start.5 = (bf16[88,256]{1,0:T(8,128)(2,1)S(1)}, bf16[88,256]{1,0:T(8,128)(2,1)S(1)}, u32[]{:S(2)}, u32[]{:S(2)}) collective-permute-start(bf16[88,256]{1,0:T(8,128)(2,1)S(1)} %concatenate.19), channel_id=1, source_target_pairs={{48,0},{64,16},{144,32},{224,48},{16,64},{96,80},{176,96},{192,112... | collective-permute-start | bytes 135176 | tf_op jit(solution)/shard_map/ppermute | solution.py:271
  5.8 3.2 %collective-permute-done.5 = bf16[88,256]{1,0:T(8,128)(2,1)S(1)} collective-permute-done((bf16[88,256]{1,0:T(8,128)(2,1)S(1)}, bf16[88,256]{1,0:T(8,128)(2,1)S(1)}, u32[]{:S(2)}, u32[]{:S(2)}) %collective-permute-start.5) | collective-permute-done | bytes 45088 | tf_op jit(solution)/shard_map/ppermute | solution.py:271
  9.1 21.1 %all_to_all.49 = bf16[8,88,256]{2,1,0:T(8,128)(2,1)S(1)} all-to-all(bf16[8,88,256]{2,1,0:T(8,128)(2,1)S(1)} %broadcast_in_dim.123), channel_id=1, replica_groups={{0,4,8,12,128,132,136,140},{1,5,9,13,129,133,137,141},{2,6,10,14,130,13..., dimensions={0} | all-to-all | bytes 720896 | tf_op jit(solution)/shard_map/all_to_all | solution.py:252
  30.3 20.6 %all_to_all.50 = bf16[4,8,88,256]{3,2,1,0:T(8,128)(2,1)S(1)} all-to-all(bf16[4,8,88,256]{3,2,1,0:T(8,128)(2,1)S(1)} %broadcast_in_dim.124), channel_id=1, replica_groups={{0,1,2,3},{4,5,6,7},{8,9,10,11},{12,13,14,15},{16,17,18,19},{20,21,22,2..., dimensions={0} | all-to-all | bytes 2883584 | tf_op jit(solution)/shard_map/all_to_all | solution.py:252
  51.8 3.2 %shard_map.127 = s16[1248,256]{1,0:T(8,128)(2,1)S(1)} custom-call(bf16[2374,1280]{1,0:T(8,128)(2,1)} %bitcast.94, bf16[1280,256]{1,0:T(8,128)(2,1)S(1)} %bitcast.91, f32[1,256]{1,0:T(1,128)S(1)} %slice.145.sum_ref), custom_call_target="tpu_custom_call" | custom-call | flops 777912320 | bytes 12154880 | tf_op jit(solution)/shard_map/pallas_call | solution.py:81
  55.0 2.5 %collective-permute-start.12 = (s16[1248,256]{1,0:T(8,128)(2,1)S(1)}, s16[1248,256]{1,0:T(8,128)(2,1)S(1)}, u32[]{:S(2)}, u32[]{:S(2)}) collective-permute-start(s16[1248,256]{1,0:T(8,128)(2,1)S(1)} %shard_map.127), channel_id=1, source_target_pairs={{0,16},{16,32},{32,48},{48,0},{64,112},{80,64},{96,80},{112,96},{1... | collective-permute-start | bytes 1916936 | tf_op jit(solution)/shard_map/ppermute | solution.py:279
  57.5 3.0 %shard_map.124 = s16[1248,256]{1,0:T(8,128)(2,1)S(1)} custom-call(bf16[2374,1280]{1,0:T(8,128)(2,1)} %bitcast.95, bf16[1280,256]{1,0:T(8,128)(2,1)S(1)} %bitcast.92, f32[1,256]{1,0:T(1,128)S(1)} %slice.145.sum_ref), custom_call_target="tpu_custom_call" | custom-call | flops 777912320 | bytes 12154880 | tf_op jit(solution)/shard_map/pallas_call | solution.py:81
  62.0 2.0 %shard_map.122.part_ref = f32[2400,256]{1,0:T(8,128)S(1)} custom-call(bf16[2374,1280]{1,0:T(8,128)(2,1)S(1)} %bitcast.101, bf16[1280,256]{1,0:T(8,128)(2,1)S(1)} %get-tuple-element.474.x_ref), custom_call_target="tpu_custom_call" | custom-call | flops 1555824640 | bytes 6077440 | tf_op jit(solution)/shard_map/pallas_call | solution.py:125
  64.0 2.0 %shard_map.123.part_ref = f32[2400,256]{1,0:T(8,128)S(1)} custom-call(bf16[2374,1280]{1,0:T(8,128)(2,1)S(1)} %bitcast.102, bf16[1280,256]{1,0:T(8,128)(2,1)S(1)} %collective-permute-done.7.x_ref), custom_call_target="tpu_custom_call" | custom-call | flops 1555824640 | bytes 6077440 | tf_op jit(solution)/shard_map/pallas_call | solution.py:125
  67.3 1.9 %collective-permute-start.13 = (s16[1248,256]{1,0:T(8,128)(2,1)}, s16[1248,256]{1,0:T(8,128)(2,1)}, u32[]{:S(2)}, u32[]{:S(2)}) collective-permute-start(s16[1248,256]{1,0:T(8,128)(2,1)} %shard_map.128), channel_id=1, source_target_pairs={{0,16},{16,32},{32,48},{48,0},{64,112},{80,64},{96,80},{112,96},{1... | collective-permute-start | bytes 1916936 | tf_op jit(solution)/shard_map/ppermute | solution.py:279
  69.2 3.1 %collective-permute-done.9.arrived_ref = s16[1248,256]{1,0:T(8,128)(2,1)S(1)} collective-permute-done((s16[1248,256]{1,0:T(8,128)(2,1)S(1)}, s16[1248,256]{1,0:T(8,128)(2,1)S(1)}, u32[]{:S(2)}, u32[]{:S(2)}) %collective-permute-start.9) | collective-permute-done | bytes 639008 | tf_op jit(solution)/shard_map/ppermute | solution.py:279
  73.6 2.5 %collective-permute-start.10 = (s16[1248,256]{1,0:T(8,128)(2,1)}, s16[1248,256]{1,0:T(8,128)(2,1)}, u32[]{:S(2)}, u32[]{:S(2)}) collective-permute-start(s16[1248,256]{1,0:T(8,128)(2,1)} %shard_map.125), channel_id=1, source_target_pairs={{0,16},{16,32},{32,48},{48,0},{64,112},{80,64},{96,80},{112,96},{1... | collective-permute-start | bytes 1916936 | tf_op jit(solution)/shard_map/ppermute | solution.py:279
  77.2 2.0 %collective-permute-done.13.arrived_ref = s16[1248,256]{1,0:T(8,128)(2,1)} collective-permute-done((s16[1248,256]{1,0:T(8,128)(2,1)}, s16[1248,256]{1,0:T(8,128)(2,1)}, u32[]{:S(2)}, u32[]{:S(2)}) %collective-permute-start.13) | collective-permute-done | bytes 639008 | tf_op jit(solution)/shard_map/ppermute | solution.py:279
  79.3 2.4 %shard_map.129 = s16[1248,256]{1,0:T(8,128)(2,1)} custom-call(f32[2400,256]{1,0:T(8,128)S(1)} %shard_map.123.part_ref, f32[1,256]{1,0:T(1,128)S(1)} %get-tuple-element.495.sum_ref, s16[1248,256]{1,0:T(8,128)(2,1)} %collective-permute-done.13.arrived_ref), custom_call_target="tpu_custom_call" | custom-call | flops 2555904 | bytes 2555904 | tf_op jit(solution)/shard_map/pallas_call | solution.py:107
  81.6 2.5 %collective-permute-start.14 = (s16[1248,256]{1,0:T(8,128)(2,1)}, s16[1248,256]{1,0:T(8,128)(2,1)}, u32[]{:S(2)}, u32[]{:S(2)}) collective-permute-start(s16[1248,256]{1,0:T(8,128)(2,1)} %shard_map.129), channel_id=1, source_target_pairs={{0,16},{16,32},{32,48},{48,0},{64,112},{80,64},{96,80},{112,96},{1... | collective-permute-start | bytes 1916936 | tf_op jit(solution)/shard_map/ppermute | solution.py:279
  84.1 2.0 %collective-permute-done.10.arrived_ref = s16[1248,256]{1,0:T(8,128)(2,1)} collective-permute-done((s16[1248,256]{1,0:T(8,128)(2,1)}, s16[1248,256]{1,0:T(8,128)(2,1)}, u32[]{:S(2)}, u32[]{:S(2)}) %collective-permute-start.10) | collective-permute-done | bytes 639008 | tf_op jit(solution)/shard_map/ppermute | solution.py:279
  86.1 2.4 %shard_map.126 = s16[1248,256]{1,0:T(8,128)(2,1)} custom-call(f32[2400,256]{1,0:T(8,128)S(1)} %shard_map.123.part_ref, f32[1,256]{1,0:T(1,128)S(1)} %get-tuple-element.495.sum_ref, s16[1248,256]{1,0:T(8,128)(2,1)} %collective-permute-done.10.arrived_ref), custom_call_target="tpu_custom_call" | custom-call | flops 2555904 | bytes 2555904 | tf_op jit(solution)/shard_map/pallas_call | solution.py:107
  88.5 2.5 %collective-permute-start.11 = (s16[1248,256]{1,0:T(8,128)(2,1)}, s16[1248,256]{1,0:T(8,128)(2,1)S(1)}, u32[]{:S(2)}, u32[]{:S(2)}) collective-permute-start(s16[1248,256]{1,0:T(8,128)(2,1)} %shard_map.126), channel_id=1, source_target_pairs={{0,16},{16,32},{32,48},{48,0},{64,112},{80,64},{96,80},{112,96},{1... | collective-permute-start | bytes 1916936 | tf_op jit(solution)/shard_map/ppermute | solution.py:279
  92.0 3.8 %shard_map.121.base_ref = f32[2400,256]{1,0:T(8,128)S(1)} custom-call(bf16[2374,1280]{1,0:T(8,128)(2,1)} %bitcast.96, bf16[1280,256]{1,0:T(8,128)(2,1)S(1)} %get-tuple-element.475.x_ref), custom_call_target="tpu_custom_call" | custom-call | flops 1555824640 | bytes 6077440 | tf_op jit(solution)/shard_map/pallas_call | solution.py:125
  95.8 4.0 %collective-permute-done.11.a_ref = s16[1248,256]{1,0:T(8,128)(2,1)S(1)} collective-permute-done((s16[1248,256]{1,0:T(8,128)(2,1)}, s16[1248,256]{1,0:T(8,128)(2,1)S(1)}, u32[]{:S(2)}, u32[]{:S(2)}) %collective-permute-start.11) | collective-permute-done | bytes 639008 | tf_op jit(solution)/shard_map/ppermute | solution.py:279
  99.8 3.1 %shard_map.130 = (bf16[2374,256]{1,0:T(8,128)(2,1)S(1)}, bf16[64,2374]{1,0:T(8,128)(2,1)S(1)}, f32[5,256]{1,0:T(8,128)S(1)}) custom-call(f32[2400,256]{1,0:T(8,128)S(1)} %shard_map.121.base_ref, s16[1248,256]{1,0:T(8,128)(2,1)S(1)} %collective-permute-done.11.a_ref, s16[1248,256]{1,0:T(8,128)(2,1)} %collective-permute-done.14.b_ref, ...), custom_call_target="tpu_custom_call" | custom-call | flops 77791232 | bytes 6077440 | tf_op jit(solution)/shard_map/pallas_call | solution.py:179
  103.6 5.9 %all-to-all-start.4 = ((f32[64,4,256]{2,1,0:T(4,128)}), f32[64,4,256]{2,1,0:T(4,128)S(1)}, u32[]{:S(2)}, u32[]{:S(2)}) async-start(f32[64,4,256]{2,1,0:T(4,128)} %broadcast_in_dim.128), calls=%async_computation.4 | async-start | bytes 524288 | tf_op jit(solution)/shard_map/all_to_all | solution.py:252
  110.4 1.8 collective-permute-start.16
  112.2 10.1 %all-to-all-done.4 = f32[64,4,256]{2,1,0:T(4,128)S(1)} async-done(((f32[64,4,256]{2,1,0:T(4,128)}), f32[64,4,256]{2,1,0:T(4,128)S(1)}, u32[]{:S(2)}, u32[]{:S(2)}) %all-to-all-start.4) | async-done | bytes 262176 | tf_op jit(solution)/shard_map/all_to_all | solution.py:252
  124.7 6.2 %all-to-all-start.5 = ((f32[4,1,256]{2,1,0:T(1,128)}), f32[4,1,256]{2,1,0:T(1,128)S(1)}, u32[]{:S(2)}, u32[]{:S(2)}) async-start(f32[4,1,256]{2,1,0:T(1,128)} %reshape.235), calls=%async_computation.5 | async-start | bytes 8192 | tf_op jit(solution)/shard_map/all_to_all | solution.py:252
  132.2 1.6 all-to-all-done.5
  135.3 2.7 %collective-permute-done.17.r2 = bf16[64,2374]{1,0:T(8,128)(2,1)S(1)} collective-permute-done((bf16[64,2374]{1,0:T(8,128)(2,1)S(1)}, bf16[64,2374]{1,0:T(8,128)(2,1)S(1)}, u32[]{:S(2)}, u32[]{:S(2)}) %collective-permute-start.17) | collective-permute-done | bytes 303904 | tf_op jit(solution)/shard_map/ppermute | solution.py:353
  137.9 6.7 %shard_map.131 = (bf16[2,640,128]{2,1,0:T(8,128)(2,1)S(1)}, bf16[2,640,128]{2,1,0:T(8,128)(2,1)S(1)}) custom-call(s32[1]{0:T(128)} %bitcast.13.core_ref, bf16[64,2374]{1,0:T(8,128)(2,1)S(1)} %collective-permute-done.16.r0, bf16[64,2374]{1,0:T(8,128)(2,1)S(1)} %collective-permute-done.15.r1, bf16[64,2374]{1,0:T(8,128)(2,1)S(1)} %collective-permute-done.17.r2, ...), custom_call_target="tpu_custom_call" | custom-call | flops 1555824640 | bytes 12154880 | tf_op jit(solution)/shard_map/pallas_call | solution.py:229
  147.2 7.1 %all-to-all-start.6 = ((bf16[32,40,128]{2,1,0:T(8,128)(2,1)}), bf16[32,40,128]{2,1,0:T(8,128)(2,1)S(1)}, u32[]{:S(2)}, u32[]{:S(2)}) async-start(bf16[32,40,128]{2,1,0:T(8,128)(2,1)} %bitcast.20), calls=%async_computation.6 | async-start | bytes 655360 | tf_op jit(solution)/shard_map/all_to_all | solution.py:364
  154.3 14.6 %all-to-all-done.6 = bf16[32,40,128]{2,1,0:T(8,128)(2,1)S(1)} async-done(((bf16[32,40,128]{2,1,0:T(8,128)(2,1)}), bf16[32,40,128]{2,1,0:T(8,128)(2,1)S(1)}, u32[]{:S(2)}, u32[]{:S(2)}) %all-to-all-start.6) | async-done | bytes 327712 | tf_op jit(solution)/shard_map/all_to_all | solution.py:364
  169.0 3.2 %collective-permute-start.19 = (f32[80,64]{1,0:T(8,128)S(1)}, f32[80,64]{1,0:T(8,128)S(1)}, u32[]{:S(2)}, u32[]{:S(2)}) collective-permute-start(f32[80,64]{1,0:T(8,128)S(1)} %pad_maximum_fusion.1), channel_id=1, source_target_pairs={{0,48},{16,64},{32,144},{48,224},{64,16},{80,96},{96,176},{112,192... | collective-permute-start | bytes 61448 | tf_op jit(solution)/shard_map/ppermute | solution.py:369
  173.5 3.9 %collective-permute-done.19 = f32[80,64]{1,0:T(8,128)S(1)} collective-permute-done((f32[80,64]{1,0:T(8,128)S(1)}, f32[80,64]{1,0:T(8,128)S(1)}, u32[]{:S(2)}, u32[]{:S(2)}) %collective-permute-start.19) | collective-permute-done | bytes 20512 | tf_op jit(solution)/shard_map/ppermute | solution.py:369
  (92 shorter events, 19.4 us)
Async XLA Ops:
  2.2 6.8 %collective-permute-start.5 = (bf16[88,256]{1,0:T(8,128)(2,1)S(1)}, bf16[88,256]{1,0:T(8,128)(2,1)S(1)}, u32[]{:S(2)}, u32[]{:S(2)}) collective-permute-start(bf16[88,256]{1,0:T(8,128)(2,1)S(1)} %concatenate.19), channel_id=1, source_target_pairs={{48,0},{64,16},{144,32},{224,48},{16,64},{96,80},{176,96},{192,112... | collective-permute-start | bytes 135176 | tf_op jit(solution)/shard_map/ppermute | solution.py:271
  51.2 9.6 %collective-permute-start.6 = (bf16[1280,256]{1,0:T(8,128)(2,1)S(1)}, bf16[1280,256]{1,0:T(8,128)(2,1)}, u32[]{:S(2)}, u32[]{:S(2)}) collective-permute-start(bf16[1280,256]{1,0:T(8,128)(2,1)S(1)} %bitcast.106), channel_id=1, source_target_pairs={{0,64},{64,0},{128,192},{192,128},{1,65},{65,1},{129,193},{193,129... | collective-permute-start | bytes 1966088 | tf_op jit(solution)/shard_map/ppermute | solution.py:284
  51.3 12.7 %collective-permute-start.7 = (bf16[1280,256]{1,0:T(8,128)(2,1)S(1)}, bf16[1280,256]{1,0:T(8,128)(2,1)S(1)}, u32[]{:S(2)}, u32[]{:S(2)}) collective-permute-start(bf16[1280,256]{1,0:T(8,128)(2,1)S(1)} %bitcast.90), channel_id=1, source_target_pairs={{0,64},{64,0},{128,192},{192,128},{1,65},{65,1},{129,193},{193,129... | collective-permute-start | bytes 1966088 | tf_op jit(solution)/shard_map/ppermute | solution.py:285
  51.8 10.2 %slice-start = ((s8[6082560]{0:T(1024)(128)(4,1)}), s8[4194304]{0:T(1024)(128)(4,1)S(1)}, s32[]{:S(2)}) async-start(s8[6082560]{0:T(1024)(128)(4,1)} %bitcast.99), calls=%async_computation.7 | async-start | bytes 8388608
  55.0 7.0 %slice-start.1 = ((s8[6082560]{0:T(1024)(128)(4,1)}), s8[1888256]{0:T(1024)(128)(4,1)S(1)}, s32[]{:S(2)}) async-start(s8[6082560]{0:T(1024)(128)(4,1)} %bitcast.99), calls=%async_computation.8 | async-start | bytes 3776512
  55.0 11.0 %collective-permute-start.12 = (s16[1248,256]{1,0:T(8,128)(2,1)S(1)}, s16[1248,256]{1,0:T(8,128)(2,1)S(1)}, u32[]{:S(2)}, u32[]{:S(2)}) collective-permute-start(s16[1248,256]{1,0:T(8,128)(2,1)S(1)} %shard_map.127), channel_id=1, source_target_pairs={{0,16},{16,32},{32,48},{48,0},{64,112},{80,64},{96,80},{112,96},{1... | collective-permute-start | bytes 1916936 | tf_op jit(solution)/shard_map/ppermute | solution.py:279
  60.5 11.8 %collective-permute-start.9 = (s16[1248,256]{1,0:T(8,128)(2,1)S(1)}, s16[1248,256]{1,0:T(8,128)(2,1)S(1)}, u32[]{:S(2)}, u32[]{:S(2)}) collective-permute-start(s16[1248,256]{1,0:T(8,128)(2,1)S(1)} %shard_map.124), channel_id=1, source_target_pairs={{0,16},{16,32},{32,48},{48,0},{64,112},{80,64},{96,80},{112,96},{1... | collective-permute-start | bytes 1916936 | tf_op jit(solution)/shard_map/ppermute | solution.py:279
  60.8 5.2 %collective-permute-start.8 = (f32[2,256]{1,0:T(2,128)S(1)}, f32[2,256]{1,0:T(2,128)S(1)}, u32[]{:S(2)}, u32[]{:S(2)}) collective-permute-start(f32[2,256]{1,0:T(2,128)S(1)} %convert_reduce_fusion.2), channel_id=1, source_target_pairs={{0,64},{64,0},{128,192},{192,128},{1,65},{65,1},{129,193},{193,129... | collective-permute-start | bytes 6152 | tf_op jit(solution)/shard_map/ppermute | solution.py:287
  67.3 8.8 %copy-start.1 = (s32[256]{0:T(256)S(1)}, s32[256]{0:T(256)}, u32[]{:S(2)}) copy-start(s32[256]{0:T(256)} %param.20) | copy-start | bytes 3076
  67.3 12.0 %collective-permute-start.13 = (s16[1248,256]{1,0:T(8,128)(2,1)}, s16[1248,256]{1,0:T(8,128)(2,1)}, u32[]{:S(2)}, u32[]{:S(2)}) collective-permute-start(s16[1248,256]{1,0:T(8,128)(2,1)} %shard_map.128), channel_id=1, source_target_pairs={{0,16},{16,32},{32,48},{48,0},{64,112},{80,64},{96,80},{112,96},{1... | collective-permute-start | bytes 1916936 | tf_op jit(solution)/shard_map/ppermute | solution.py:279
  73.6 12.5 %collective-permute-start.10 = (s16[1248,256]{1,0:T(8,128)(2,1)}, s16[1248,256]{1,0:T(8,128)(2,1)}, u32[]{:S(2)}, u32[]{:S(2)}) collective-permute-start(s16[1248,256]{1,0:T(8,128)(2,1)} %shard_map.125), channel_id=1, source_target_pairs={{0,16},{16,32},{32,48},{48,0},{64,112},{80,64},{96,80},{112,96},{1... | collective-permute-start | bytes 1916936 | tf_op jit(solution)/shard_map/ppermute | solution.py:279
  81.6 9.3 %copy-start.2 = (s32[256]{0:T(256)S(1)}, s32[256]{0:T(256)}, u32[]{:S(2)}) copy-start(s32[256]{0:T(256)} %param.21) | copy-start | bytes 3076
  81.6 9.3 %copy-start.3 = (f32[256]{0:T(256)S(1)}, f32[256]{0:T(256)}, u32[]{:S(2)}) copy-start(f32[256]{0:T(256)} %param.23) | copy-start | bytes 3076
  81.6 10.3 %copy-start.4 = (s32[256]{0:T(256)S(1)}, s32[256]{0:T(256)}, u32[]{:S(2)}) copy-start(s32[256]{0:T(256)} %param.19) | copy-start | bytes 3076
  81.6 14.2 %collective-permute-start.14 = (s16[1248,256]{1,0:T(8,128)(2,1)}, s16[1248,256]{1,0:T(8,128)(2,1)}, u32[]{:S(2)}, u32[]{:S(2)}) collective-permute-start(s16[1248,256]{1,0:T(8,128)(2,1)} %shard_map.129), channel_id=1, source_target_pairs={{0,16},{16,32},{32,48},{48,0},{64,112},{80,64},{96,80},{112,96},{1... | collective-permute-start | bytes 1916936 | tf_op jit(solution)/shard_map/ppermute | solution.py:279
  88.5 11.3 %collective-permute-start.11 = (s16[1248,256]{1,0:T(8,128)(2,1)}, s16[1248,256]{1,0:T(8,128)(2,1)S(1)}, u32[]{:S(2)}, u32[]{:S(2)}) collective-permute-start(s16[1248,256]{1,0:T(8,128)(2,1)} %shard_map.126), channel_id=1, source_target_pairs={{0,16},{16,32},{32,48},{48,0},{64,112},{80,64},{96,80},{112,96},{1... | collective-permute-start | bytes 1916936 | tf_op jit(solution)/shard_map/ppermute | solution.py:279
  99.8 9.8 %copy-start.6 = (f32[4]{0:T(128)S(1)}, f32[4]{0:T(128)}, u32[]{:S(2)}) copy-start(f32[4]{0:T(128)} %constant.225.clone) | copy-start | bytes 52
  102.9 19.7 %copy-start.5 = (f32[256]{0:T(256)S(1)}, f32[256]{0:T(256)}, u32[]{:S(2)}) copy-start(f32[256]{0:T(256)} %param.22) | copy-start | bytes 3076
  103.6 18.7 %all-to-all-start.4 = ((f32[64,4,256]{2,1,0:T(4,128)}), f32[64,4,256]{2,1,0:T(4,128)S(1)}, u32[]{:S(2)}, u32[]{:S(2)}) async-start(f32[64,4,256]{2,1,0:T(4,128)} %broadcast_in_dim.128), calls=%async_computation.4 | async-start | bytes 524288 | tf_op jit(solution)/shard_map/all_to_all | solution.py:252
  109.7 14.3 %collective-permute-start.15 = (bf16[64,2374]{1,0:T(8,128)(2,1)S(1)}, bf16[64,2374]{1,0:T(8,128)(2,1)S(1)}, u32[]{:S(2)}, u32[]{:S(2)}) collective-permute-start(bf16[64,2374]{1,0:T(8,128)(2,1)S(1)} %get-tuple-element.304.r3), channel_id=1, source_target_pairs={{0,48},{16,0},{32,16},{48,32},{1,49},{17,1},{33,17},{49,33},{2,50}... | collective-permute-start | bytes 911624 | tf_op jit(solution)/shard_map/ppermute | solution.py:313
  110.4 13.6 %collective-permute-start.16 = (bf16[64,2374]{1,0:T(8,128)(2,1)S(1)}, bf16[64,2374]{1,0:T(8,128)(2,1)S(1)}, u32[]{:S(2)}, u32[]{:S(2)}) collective-permute-start(bf16[64,2374]{1,0:T(8,128)(2,1)S(1)} %get-tuple-element.304.r3), channel_id=1, source_target_pairs={{0,16},{16,32},{32,48},{48,0},{1,17},{17,33},{33,49},{49,1},{2,18}... | collective-permute-start | bytes 911624 | tf_op jit(solution)/shard_map/ppermute | solution.py:312
  124.7 9.2 %all-to-all-start.5 = ((f32[4,1,256]{2,1,0:T(1,128)}), f32[4,1,256]{2,1,0:T(1,128)S(1)}, u32[]{:S(2)}, u32[]{:S(2)}) async-start(f32[4,1,256]{2,1,0:T(1,128)} %reshape.235), calls=%async_computation.5 | async-start | bytes 8192 | tf_op jit(solution)/shard_map/all_to_all | solution.py:252
  131.0 7.0 %collective-permute-start.17 = (bf16[64,2374]{1,0:T(8,128)(2,1)S(1)}, bf16[64,2374]{1,0:T(8,128)(2,1)S(1)}, u32[]{:S(2)}, u32[]{:S(2)}) collective-permute-start(bf16[64,2374]{1,0:T(8,128)(2,1)S(1)} %broadcast_select_fusion.3), channel_id=1, source_target_pairs={{0,16},{16,32},{32,48},{48,0},{64,112},{80,64},{96,80},{112,96},{1... | collective-permute-start | bytes 911624 | tf_op jit(solution)/shard_map/ppermute | solution.py:353
  144.7 1.7 collective-permute-start.18
  147.2 21.7 %all-to-all-start.6 = ((bf16[32,40,128]{2,1,0:T(8,128)(2,1)}), bf16[32,40,128]{2,1,0:T(8,128)(2,1)S(1)}, u32[]{:S(2)}, u32[]{:S(2)}) async-start(bf16[32,40,128]{2,1,0:T(8,128)(2,1)} %bitcast.20), calls=%async_computation.6 | async-start | bytes 655360 | tf_op jit(solution)/shard_map/all_to_all | solution.py:364
  169.0 8.3 %collective-permute-start.19 = (f32[80,64]{1,0:T(8,128)S(1)}, f32[80,64]{1,0:T(8,128)S(1)}, u32[]{:S(2)}, u32[]{:S(2)}) collective-permute-start(f32[80,64]{1,0:T(8,128)S(1)} %pad_maximum_fusion.1), channel_id=1, source_target_pairs={{0,48},{16,64},{32,144},{48,224},{64,16},{80,96},{96,176},{112,192... | collective-permute-start | bytes 61448 | tf_op jit(solution)/shard_map/ppermute | solution.py:369
  177.5 0.8 copy-start
where the time goes:
time: 180 us; the launch traced here: 179 us
  waiting for transfers between devices  48.9 us (27%)
  starting transfers between devices  42.6 us (24%)
  blocking collectives  41.8 us (23%)
  Pallas kernels  31 us (17%)
  other arithmetic  8.52 us (5%)
  local copies, waits for them, and re-layouts  3.45 us (2%)
  between operations  2.36 us (1%)
    all_to_all x2, blocking collectives, share(): lax.all_to_all(copies, axes, 0, 0, tiled=True, axis_index_groups=groups)  41.8 us
    all_to_all x1, waiting for transfers between devices, chunk_grad(): lax.all_to_all(part, (SECTION, VOCAB), 0, 0, tiled=True, axis_index_group...  14.6 us
    all_to_all x2, starting transfers between devices, share(): lax.all_to_all(copies, axes, 0, 0, tiled=True, axis_index_groups=groups)  12.2 us
    ppermute x6, starting transfers between devices, send(): return lax.ppermute(part, (SECTION, DP), STEP)  12.1 us
    all_to_all x2, waiting for transfers between devices, share(): lax.all_to_all(copies, axes, 0, 0, tiled=True, axis_index_groups=groups)  11.8 us
    ppermute x6, waiting for transfers between devices, send(): return lax.ppermute(part, (SECTION, DP), STEP)  11.1 us
    pallas_call x3, Pallas kernels, base(): pl.pallas_call(functools.partial(base_kernel, rows), out_shape=jax.ShapeD...  7.82 us
    pallas_call x4, Pallas kernels, message(): pl.pallas_call(functools.partial(message_kernel, half), out_shape=jax.Sha...  7.25 us
  transfers between devices with their start and end apart: 18, of which 11 were waited for; matrix products, arithmetic and copies ran while one was open for 4% of the time, Pallas kernels for 12%

commit v1 on v0

--- a/solution.py
+++ b/solution.py
@@ -13,9 +13,9 @@
 GPD = 8
 CHUNK = 64
 SHARE = 80
-TILE = 400
+TILE = 1200
 EXTRA = 16
-HALF_TILES = 3
+HALF_TILES = 1
 BIG = 32000.0
 REL = (3, 1, 2, 0)
 SECTION, DP, VOCAB = "section", "dp", "vocab"
@@ -30,7 +30,7 @@
 SPREAD = tuple((d * 4 + (d + REL[s]) % 4, s * 4 + d) for s in range(4) for d in range(4))
 COLLECT = tuple((b, a) for a, b in SPREAD)
 SMALL = pltpu.CompilerParams(vmem_limit_bytes=10 * 1024 * 1024)
-LARGE = pltpu.CompilerParams(vmem_limit_bytes=20 * 1024 * 1024)
+LARGE = pltpu.CompilerParams(vmem_limit_bytes=15 * 1024 * 1024)
 
 
 def decode(block):
@@ -195,14 +195,11 @@
     @pl.when(pl.program_id(0) == 0)
     def _():
         for t, ref in enumerate((r0, r1, r2, r3)):
-            @pl.loop(0, CHUNK // 16)
-            def _(step, t=t, ref=ref):
-                here = pl.ds(pl.multiple_of(step * 16, 16), 16)
-                factor = factor_ref[pl.ds(pl.multiple_of(t * CHUNK + step * 16, 16), 16), :]
-                index = lax.broadcasted_iota(i32, (16, rows), 1)
-                hard = jnp.where(index == factor[:, 2:3].astype(i32), factor[:, 1:2], 0.0)
-                value = ref[here, :].astype(f32) * factor[:, 0:1] + hard
-                left[pl.ds(pl.multiple_of(t * CHUNK + step * 16, 16), 16), :] = value.astype(bf16)
+            factor = factor_ref[t * CHUNK : (t + 1) * CHUNK, :]
+            index = lax.broadcasted_iota(i32, (CHUNK, rows), 1)
+            hard = jnp.where(index == factor[:, 2:3].astype(i32), factor[:, 1:2], 0.0)
+            value = ref[...].astype(f32) * factor[:, 0:1] + hard
+            left[t * CHUNK : (t + 1) * CHUNK, :] = value.astype(bf16)
 
     out = jnp.dot(left[...], head_ref[...], preferred_element_type=f32)
     for t in range(4):

time: 180 us -> 178 us (0.989)
  no operation moved by 1% of the time
where the time goes in v1:
time: 178 us; the launch traced here: 177 us
  waiting for transfers between devices  47.9 us (27%)
  starting transfers between devices  42.3 us (24%)
  blocking collectives  41.8 us (23%)
  Pallas kernels  30.5 us (17%)
  other arithmetic  8.52 us (5%)
  local copies, waits for them, and re-layouts  3.45 us (2%)
  between operations  2.37 us (1%)
    all_to_all x2, blocking collectives, share(): lax.all_to_all(copies, axes, 0, 0, tiled=True, axis_index_groups=groups)  41.8 us
    all_to_all x1, waiting for transfers between devices, chunk_grad(): lax.all_to_all(part, (SECTION, VOCAB), 0, 0, tiled=True, axis_index_group...  14.6 us
    all_to_all x2, starting transfers between devices, share(): lax.all_to_all(copies, axes, 0, 0, tiled=True, axis_index_groups=groups)  12.4 us
    ppermute x6, starting transfers between devices, send(): return lax.ppermute(part, (SECTION, DP), STEP)  11.8 us
    all_to_all x2, waiting for transfers between devices, share(): lax.all_to_all(copies, axes, 0, 0, tiled=True, axis_index_groups=groups)  11.8 us
    ppermute x6, waiting for transfers between devices, send(): return lax.ppermute(part, (SECTION, DP), STEP)  10.1 us
    pallas_call x3, Pallas kernels, base(): pl.pallas_call(functools.partial(base_kernel, rows), out_shape=jax.ShapeD...  7.81 us
    pallas_call x4, Pallas kernels, message(): pl.pallas_call(functools.partial(message_kernel, half), out_shape=jax.Sha...  7.41 us
  transfers between devices with their start and end apart: 18, of which 11 were waited for; matrix products, arithmetic and copies ran while one was open for 4% of the time, Pallas kernels for 12%

profile of v1, /device:TPU:16, one launch (start us, length us, event | category | flops | bytes accessed | tf_op | source)
XLA Modules:
  0.0 177.1 jit_solution(6213184610219729473)
XLA Ops:
  2.2 3.6 %collective-permute-start.5 = (bf16[88,256]{1,0:T(8,128)(2,1)S(1)}, bf16[88,256]{1,0:T(8,128)(2,1)S(1)}, u32[]{:S(2)}, u32[]{:S(2)}) collective-permute-start(bf16[88,256]{1,0:T(8,128)(2,1)S(1)} %concatenate.19), channel_id=1, source_target_pairs={{48,0},{64,16},{144,32},{224,48},{16,64},{96,80},{176,96},{192,112... | collective-permute-start | bytes 135176 | tf_op jit(solution)/shard_map/ppermute | solution.py:268
  5.8 3.2 %collective-permute-done.5 = bf16[88,256]{1,0:T(8,128)(2,1)S(1)} collective-permute-done((bf16[88,256]{1,0:T(8,128)(2,1)S(1)}, bf16[88,256]{1,0:T(8,128)(2,1)S(1)}, u32[]{:S(2)}, u32[]{:S(2)}) %collective-permute-start.5) | collective-permute-done | bytes 45088 | tf_op jit(solution)/shard_map/ppermute | solution.py:268
  9.1 21.1 %all_to_all.49 = bf16[8,88,256]{2,1,0:T(8,128)(2,1)S(1)} all-to-all(bf16[8,88,256]{2,1,0:T(8,128)(2,1)S(1)} %broadcast_in_dim.123), channel_id=1, replica_groups={{0,4,8,12,128,132,136,140},{1,5,9,13,129,133,137,141},{2,6,10,14,130,13..., dimensions={0} | all-to-all | bytes 720896 | tf_op jit(solution)/shard_map/all_to_all | solution.py:249
  30.3 20.6 %all_to_all.50 = bf16[4,8,88,256]{3,2,1,0:T(8,128)(2,1)S(1)} all-to-all(bf16[4,8,88,256]{3,2,1,0:T(8,128)(2,1)S(1)} %broadcast_in_dim.124), channel_id=1, replica_groups={{0,1,2,3},{4,5,6,7},{8,9,10,11},{12,13,14,15},{16,17,18,19},{20,21,22,2..., dimensions={0} | all-to-all | bytes 2883584 | tf_op jit(solution)/shard_map/all_to_all | solution.py:249
  51.8 3.2 %shard_map.127 = s16[1216,256]{1,0:T(8,128)(2,1)S(1)} custom-call(bf16[2374,1280]{1,0:T(8,128)(2,1)} %bitcast.94, bf16[1280,256]{1,0:T(8,128)(2,1)S(1)} %bitcast.91, f32[1,256]{1,0:T(1,128)S(1)} %slice.145.sum_ref), custom_call_target="tpu_custom_call" | custom-call | flops 777912320 | bytes 12154880 | tf_op jit(solution)/shard_map/pallas_call | solution.py:81
  55.1 2.5 %collective-permute-start.12 = (s16[1216,256]{1,0:T(8,128)(2,1)S(1)}, s16[1216,256]{1,0:T(8,128)(2,1)S(1)}, u32[]{:S(2)}, u32[]{:S(2)}) collective-permute-start(s16[1216,256]{1,0:T(8,128)(2,1)S(1)} %shard_map.127), channel_id=1, source_target_pairs={{0,16},{16,32},{32,48},{48,0},{64,112},{80,64},{96,80},{112,96},{1... | collective-permute-start | bytes 1867784 | tf_op jit(solution)/shard_map/ppermute | solution.py:276
  57.6 3.1 %shard_map.124 = s16[1216,256]{1,0:T(8,128)(2,1)S(1)} custom-call(bf16[2374,1280]{1,0:T(8,128)(2,1)} %bitcast.95, bf16[1280,256]{1,0:T(8,128)(2,1)S(1)} %bitcast.92, f32[1,256]{1,0:T(1,128)S(1)} %slice.145.sum_ref), custom_call_target="tpu_custom_call" | custom-call | flops 777912320 | bytes 12154880 | tf_op jit(solution)/shard_map/pallas_call | solution.py:81
  62.2 2.0 %shard_map.122.part_ref = f32[2400,256]{1,0:T(8,128)S(1)} custom-call(bf16[2374,1280]{1,0:T(8,128)(2,1)S(1)} %bitcast.101, bf16[1280,256]{1,0:T(8,128)(2,1)S(1)} %get-tuple-element.474.x_ref), custom_call_target="tpu_custom_call" | custom-call | flops 1555824640 | bytes 6077440 | tf_op jit(solution)/shard_map/pallas_call | solution.py:125
  64.2 2.0 %shard_map.123.part_ref = f32[2400,256]{1,0:T(8,128)S(1)} custom-call(bf16[2374,1280]{1,0:T(8,128)(2,1)S(1)} %bitcast.102, bf16[1280,256]{1,0:T(8,128)(2,1)S(1)} %collective-permute-done.7.x_ref), custom_call_target="tpu_custom_call" | custom-call | flops 1555824640 | bytes 6077440 | tf_op jit(solution)/shard_map/pallas_call | solution.py:125
  67.5 1.7 collective-permute-start.13
  69.1 2.9 %collective-permute-done.9.arrived_ref = s16[1216,256]{1,0:T(8,128)(2,1)S(1)} collective-permute-done((s16[1216,256]{1,0:T(8,128)(2,1)S(1)}, s16[1216,256]{1,0:T(8,128)(2,1)S(1)}, u32[]{:S(2)}, u32[]{:S(2)}) %collective-permute-start.9) | collective-permute-done | bytes 622624 | tf_op jit(solution)/shard_map/ppermute | solution.py:276
  73.4 2.5 %collective-permute-start.10 = (s16[1216,256]{1,0:T(8,128)(2,1)}, s16[1216,256]{1,0:T(8,128)(2,1)}, u32[]{:S(2)}, u32[]{:S(2)}) collective-permute-start(s16[1216,256]{1,0:T(8,128)(2,1)} %shard_map.125), channel_id=1, source_target_pairs={{0,16},{16,32},{32,48},{48,0},{64,112},{80,64},{96,80},{112,96},{1... | collective-permute-start | bytes 1867784 | tf_op jit(solution)/shard_map/ppermute | solution.py:276
  77.0 1.8 %collective-permute-done.13.arrived_ref = s16[1216,256]{1,0:T(8,128)(2,1)} collective-permute-done((s16[1216,256]{1,0:T(8,128)(2,1)}, s16[1216,256]{1,0:T(8,128)(2,1)}, u32[]{:S(2)}, u32[]{:S(2)}) %collective-permute-start.13) | collective-permute-done | bytes 622624 | tf_op jit(solution)/shard_map/ppermute | solution.py:276
  78.8 2.4 %shard_map.129 = s16[1216,256]{1,0:T(8,128)(2,1)} custom-call(f32[2400,256]{1,0:T(8,128)S(1)} %shard_map.123.part_ref, f32[1,256]{1,0:T(1,128)S(1)} %get-tuple-element.495.sum_ref, s16[1216,256]{1,0:T(8,128)(2,1)} %collective-permute-done.13.arrived_ref), custom_call_target="tpu_custom_call" | custom-call | flops 2490368 | bytes 2490368 | tf_op jit(solution)/shard_map/pallas_call | solution.py:107
  81.2 2.5 %collective-permute-start.14 = (s16[1216,256]{1,0:T(8,128)(2,1)}, s16[1216,256]{1,0:T(8,128)(2,1)}, u32[]{:S(2)}, u32[]{:S(2)}) collective-permute-start(s16[1216,256]{1,0:T(8,128)(2,1)} %shard_map.129), channel_id=1, source_target_pairs={{0,16},{16,32},{32,48},{48,0},{64,112},{80,64},{96,80},{112,96},{1... | collective-permute-start | bytes 1867784 | tf_op jit(solution)/shard_map/ppermute | solution.py:276
  83.7 1.8 %collective-permute-done.10.arrived_ref = s16[1216,256]{1,0:T(8,128)(2,1)} collective-permute-done((s16[1216,256]{1,0:T(8,128)(2,1)}, s16[1216,256]{1,0:T(8,128)(2,1)}, u32[]{:S(2)}, u32[]{:S(2)}) %collective-permute-start.10) | collective-permute-done | bytes 622624 | tf_op jit(solution)/shard_map/ppermute | solution.py:276
  85.5 2.4 %shard_map.126 = s16[1216,256]{1,0:T(8,128)(2,1)} custom-call(f32[2400,256]{1,0:T(8,128)S(1)} %shard_map.123.part_ref, f32[1,256]{1,0:T(1,128)S(1)} %get-tuple-element.495.sum_ref, s16[1216,256]{1,0:T(8,128)(2,1)} %collective-permute-done.10.arrived_ref), custom_call_target="tpu_custom_call" | custom-call | flops 2490368 | bytes 2490368 | tf_op jit(solution)/shard_map/pallas_call | solution.py:107
  87.9 2.5 %collective-permute-start.11 = (s16[1216,256]{1,0:T(8,128)(2,1)}, s16[1216,256]{1,0:T(8,128)(2,1)S(1)}, u32[]{:S(2)}, u32[]{:S(2)}) collective-permute-start(s16[1216,256]{1,0:T(8,128)(2,1)} %shard_map.126), channel_id=1, source_target_pairs={{0,16},{16,32},{32,48},{48,0},{64,112},{80,64},{96,80},{112,96},{1... | collective-permute-start | bytes 1867784 | tf_op jit(solution)/shard_map/ppermute | solution.py:276
  91.4 3.8 %shard_map.121.base_ref = f32[2400,256]{1,0:T(8,128)S(1)} custom-call(bf16[2374,1280]{1,0:T(8,128)(2,1)} %bitcast.96, bf16[1280,256]{1,0:T(8,128)(2,1)S(1)} %get-tuple-element.475.x_ref), custom_call_target="tpu_custom_call" | custom-call | flops 1555824640 | bytes 6077440 | tf_op jit(solution)/shard_map/pallas_call | solution.py:125
  95.3 3.6 %collective-permute-done.11.a_ref = s16[1216,256]{1,0:T(8,128)(2,1)S(1)} collective-permute-done((s16[1216,256]{1,0:T(8,128)(2,1)}, s16[1216,256]{1,0:T(8,128)(2,1)S(1)}, u32[]{:S(2)}, u32[]{:S(2)}) %collective-permute-start.11) | collective-permute-done | bytes 622624 | tf_op jit(solution)/shard_map/ppermute | solution.py:276
  98.8 3.1 %shard_map.130 = (bf16[2374,256]{1,0:T(8,128)(2,1)S(1)}, bf16[64,2374]{1,0:T(8,128)(2,1)S(1)}, f32[5,256]{1,0:T(8,128)S(1)}) custom-call(f32[2400,256]{1,0:T(8,128)S(1)} %shard_map.121.base_ref, s16[1216,256]{1,0:T(8,128)(2,1)S(1)} %collective-permute-done.11.a_ref, s16[1216,256]{1,0:T(8,128)(2,1)} %collective-permute-done.14.b_ref, ...), custom_call_target="tpu_custom_call" | custom-call | flops 77791232 | bytes 6077440 | tf_op jit(solution)/shard_map/pallas_call | solution.py:179
  102.7 5.9 %all-to-all-start.4 = ((f32[64,4,256]{2,1,0:T(4,128)}), f32[64,4,256]{2,1,0:T(4,128)S(1)}, u32[]{:S(2)}, u32[]{:S(2)}) async-start(f32[64,4,256]{2,1,0:T(4,128)} %broadcast_in_dim.128), calls=%async_computation.4 | async-start | bytes 524288 | tf_op jit(solution)/shard_map/all_to_all | solution.py:249
  111.3 10.1 %all-to-all-done.4 = f32[64,4,256]{2,1,0:T(4,128)S(1)} async-done(((f32[64,4,256]{2,1,0:T(4,128)}), f32[64,4,256]{2,1,0:T(4,128)S(1)}, u32[]{:S(2)}, u32[]{:S(2)}) %all-to-all-start.4) | async-done | bytes 262176 | tf_op jit(solution)/shard_map/all_to_all | solution.py:249
  123.7 6.5 %all-to-all-start.5 = ((f32[4,1,256]{2,1,0:T(1,128)}), f32[4,1,256]{2,1,0:T(1,128)S(1)}, u32[]{:S(2)}, u32[]{:S(2)}) async-start(f32[4,1,256]{2,1,0:T(1,128)} %reshape.235), calls=%async_computation.5 | async-start | bytes 8192 | tf_op jit(solution)/shard_map/all_to_all | solution.py:249
  131.5 1.6 all-to-all-done.5
  134.6 2.7 %collective-permute-done.17.r2 = bf16[64,2374]{1,0:T(8,128)(2,1)S(1)} collective-permute-done((bf16[64,2374]{1,0:T(8,128)(2,1)S(1)}, bf16[64,2374]{1,0:T(8,128)(2,1)S(1)}, u32[]{:S(2)}, u32[]{:S(2)}) %collective-permute-start.17) | collective-permute-done | bytes 303904 | tf_op jit(solution)/shard_map/ppermute | solution.py:350
  137.2 5.8 %shard_map.131 = (bf16[2,640,128]{2,1,0:T(8,128)(2,1)S(1)}, bf16[2,640,128]{2,1,0:T(8,128)(2,1)S(1)}) custom-call(s32[1]{0:T(128)} %bitcast.13.core_ref, bf16[64,2374]{1,0:T(8,128)(2,1)S(1)} %collective-permute-done.16.r0, bf16[64,2374]{1,0:T(8,128)(2,1)S(1)} %collective-permute-done.15.r1, bf16[64,2374]{1,0:T(8,128)(2,1)S(1)} %collective-permute-done.17.r2, ...), custom_call_target="tpu_custom_call" | custom-call | flops 1555824640 | bytes 12154880 | tf_op jit(solution)/shard_map/pallas_call | solution.py:226
  143.2 1.6 collective-permute-done.18
  145.6 6.8 %all-to-all-start.6 = ((bf16[32,40,128]{2,1,0:T(8,128)(2,1)}), bf16[32,40,128]{2,1,0:T(8,128)(2,1)S(1)}, u32[]{:S(2)}, u32[]{:S(2)}) async-start(bf16[32,40,128]{2,1,0:T(8,128)(2,1)} %bitcast.20), calls=%async_computation.6 | async-start | bytes 655360 | tf_op jit(solution)/shard_map/all_to_all | solution.py:361
  152.4 14.6 %all-to-all-done.6 = bf16[32,40,128]{2,1,0:T(8,128)(2,1)S(1)} async-done(((bf16[32,40,128]{2,1,0:T(8,128)(2,1)}), bf16[32,40,128]{2,1,0:T(8,128)(2,1)S(1)}, u32[]{:S(2)}, u32[]{:S(2)}) %all-to-all-start.6) | async-done | bytes 327712 | tf_op jit(solution)/shard_map/all_to_all | solution.py:361
  167.2 3.2 %collective-permute-start.19 = (f32[80,64]{1,0:T(8,128)S(1)}, f32[80,64]{1,0:T(8,128)S(1)}, u32[]{:S(2)}, u32[]{:S(2)}) collective-permute-start(f32[80,64]{1,0:T(8,128)S(1)} %pad_maximum_fusion.1), channel_id=1, source_target_pairs={{0,48},{16,64},{32,144},{48,224},{64,16},{80,96},{96,176},{112,192... | collective-permute-start | bytes 61448 | tf_op jit(solution)/shard_map/ppermute | solution.py:366
  171.6 3.9 %collective-permute-done.19 = f32[80,64]{1,0:T(8,128)S(1)} collective-permute-done((f32[80,64]{1,0:T(8,128)S(1)}, f32[80,64]{1,0:T(8,128)S(1)}, u32[]{:S(2)}, u32[]{:S(2)}) %collective-permute-start.19) | collective-permute-done | bytes 20512 | tf_op jit(solution)/shard_map/ppermute | solution.py:366
  (92 shorter events, 19.7 us)
Async XLA Ops:
  2.2 6.8 %collective-permute-start.5 = (bf16[88,256]{1,0:T(8,128)(2,1)S(1)}, bf16[88,256]{1,0:T(8,128)(2,1)S(1)}, u32[]{:S(2)}, u32[]{:S(2)}) collective-permute-start(bf16[88,256]{1,0:T(8,128)(2,1)S(1)} %concatenate.19), channel_id=1, source_target_pairs={{48,0},{64,16},{144,32},{224,48},{16,64},{96,80},{176,96},{192,112... | collective-permute-start | bytes 135176 | tf_op jit(solution)/shard_map/ppermute | solution.py:268
  51.2 9.8 %collective-permute-start.6 = (bf16[1280,256]{1,0:T(8,128)(2,1)S(1)}, bf16[1280,256]{1,0:T(8,128)(2,1)}, u32[]{:S(2)}, u32[]{:S(2)}) collective-permute-start(bf16[1280,256]{1,0:T(8,128)(2,1)S(1)} %bitcast.106), channel_id=1, source_target_pairs={{0,64},{64,0},{128,192},{192,128},{1,65},{65,1},{129,193},{193,129... | collective-permute-start | bytes 1966088 | tf_op jit(solution)/shard_map/ppermute | solution.py:281
  51.3 12.9 %collective-permute-start.7 = (bf16[1280,256]{1,0:T(8,128)(2,1)S(1)}, bf16[1280,256]{1,0:T(8,128)(2,1)S(1)}, u32[]{:S(2)}, u32[]{:S(2)}) collective-permute-start(bf16[1280,256]{1,0:T(8,128)(2,1)S(1)} %bitcast.90), channel_id=1, source_target_pairs={{0,64},{64,0},{128,192},{192,128},{1,65},{65,1},{129,193},{193,129... | collective-permute-start | bytes 1966088 | tf_op jit(solution)/shard_map/ppermute | solution.py:282
  51.8 10.3 %slice-start = ((s8[6082560]{0:T(1024)(128)(4,1)}), s8[4194304]{0:T(1024)(128)(4,1)S(1)}, s32[]{:S(2)}) async-start(s8[6082560]{0:T(1024)(128)(4,1)} %bitcast.99), calls=%async_computation.7 | async-start | bytes 8388608
  55.1 7.1 %slice-start.1 = ((s8[6082560]{0:T(1024)(128)(4,1)}), s8[1888256]{0:T(1024)(128)(4,1)S(1)}, s32[]{:S(2)}) async-start(s8[6082560]{0:T(1024)(128)(4,1)} %bitcast.99), calls=%async_computation.8 | async-start | bytes 3776512
  55.1 11.1 %collective-permute-start.12 = (s16[1216,256]{1,0:T(8,128)(2,1)S(1)}, s16[1216,256]{1,0:T(8,128)(2,1)S(1)}, u32[]{:S(2)}, u32[]{:S(2)}) collective-permute-start(s16[1216,256]{1,0:T(8,128)(2,1)S(1)} %shard_map.127), channel_id=1, source_target_pairs={{0,16},{16,32},{32,48},{48,0},{64,112},{80,64},{96,80},{112,96},{1... | collective-permute-start | bytes 1867784 | tf_op jit(solution)/shard_map/ppermute | solution.py:276
  60.7 11.3 %collective-permute-start.9 = (s16[1216,256]{1,0:T(8,128)(2,1)S(1)}, s16[1216,256]{1,0:T(8,128)(2,1)S(1)}, u32[]{:S(2)}, u32[]{:S(2)}) collective-permute-start(s16[1216,256]{1,0:T(8,128)(2,1)S(1)} %shard_map.124), channel_id=1, source_target_pairs={{0,16},{16,32},{32,48},{48,0},{64,112},{80,64},{96,80},{112,96},{1... | collective-permute-start | bytes 1867784 | tf_op jit(solution)/shard_map/ppermute | solution.py:276
  61.0 5.2 %collective-permute-start.8 = (f32[2,256]{1,0:T(2,128)S(1)}, f32[2,256]{1,0:T(2,128)S(1)}, u32[]{:S(2)}, u32[]{:S(2)}) collective-permute-start(f32[2,256]{1,0:T(2,128)S(1)} %convert_reduce_fusion.2), channel_id=1, source_target_pairs={{0,64},{64,0},{128,192},{192,128},{1,65},{65,1},{129,193},{193,129... | collective-permute-start | bytes 6152 | tf_op jit(solution)/shard_map/ppermute | solution.py:284
  67.5 8.4 %copy-start.1 = (s32[256]{0:T(256)S(1)}, s32[256]{0:T(256)}, u32[]{:S(2)}) copy-start(s32[256]{0:T(256)} %param.20) | copy-start | bytes 3076
  67.5 11.4 %collective-permute-start.13 = (s16[1216,256]{1,0:T(8,128)(2,1)}, s16[1216,256]{1,0:T(8,128)(2,1)}, u32[]{:S(2)}, u32[]{:S(2)}) collective-permute-start(s16[1216,256]{1,0:T(8,128)(2,1)} %shard_map.128), channel_id=1, source_target_pairs={{0,16},{16,32},{32,48},{48,0},{64,112},{80,64},{96,80},{112,96},{1... | collective-permute-start | bytes 1867784 | tf_op jit(solution)/shard_map/ppermute | solution.py:276
  73.4 12.1 %collective-permute-start.10 = (s16[1216,256]{1,0:T(8,128)(2,1)}, s16[1216,256]{1,0:T(8,128)(2,1)}, u32[]{:S(2)}, u32[]{:S(2)}) collective-permute-start(s16[1216,256]{1,0:T(8,128)(2,1)} %shard_map.125), channel_id=1, source_target_pairs={{0,16},{16,32},{32,48},{48,0},{64,112},{80,64},{96,80},{112,96},{1... | collective-permute-start | bytes 1867784 | tf_op jit(solution)/shard_map/ppermute | solution.py:276
  81.2 9.2 %copy-start.2 = (s32[256]{0:T(256)S(1)}, s32[256]{0:T(256)}, u32[]{:S(2)}) copy-start(s32[256]{0:T(256)} %param.21) | copy-start | bytes 3076
  81.2 9.2 %copy-start.3 = (f32[256]{0:T(256)S(1)}, f32[256]{0:T(256)}, u32[]{:S(2)}) copy-start(f32[256]{0:T(256)} %param.23) | copy-start | bytes 3076
  81.2 10.1 %copy-start.4 = (s32[256]{0:T(256)S(1)}, s32[256]{0:T(256)}, u32[]{:S(2)}) copy-start(s32[256]{0:T(256)} %param.19) | copy-start | bytes 3076
  81.2 14.0 %collective-permute-start.14 = (s16[1216,256]{1,0:T(8,128)(2,1)}, s16[1216,256]{1,0:T(8,128)(2,1)}, u32[]{:S(2)}, u32[]{:S(2)}) collective-permute-start(s16[1216,256]{1,0:T(8,128)(2,1)} %shard_map.129), channel_id=1, source_target_pairs={{0,16},{16,32},{32,48},{48,0},{64,112},{80,64},{96,80},{112,96},{1... | collective-permute-start | bytes 1867784 | tf_op jit(solution)/shard_map/ppermute | solution.py:276
  87.9 10.9 %collective-permute-start.11 = (s16[1216,256]{1,0:T(8,128)(2,1)}, s16[1216,256]{1,0:T(8,128)(2,1)S(1)}, u32[]{:S(2)}, u32[]{:S(2)}) collective-permute-start(s16[1216,256]{1,0:T(8,128)(2,1)} %shard_map.126), channel_id=1, source_target_pairs={{0,16},{16,32},{32,48},{48,0},{64,112},{80,64},{96,80},{112,96},{1... | collective-permute-start | bytes 1867784 | tf_op jit(solution)/shard_map/ppermute | solution.py:276
  98.8 9.9 %copy-start.6 = (f32[4]{0:T(128)S(1)}, f32[4]{0:T(128)}, u32[]{:S(2)}) copy-start(f32[4]{0:T(128)} %constant.225.clone) | copy-start | bytes 52
  101.9 19.7 %copy-start.5 = (f32[256]{0:T(256)S(1)}, f32[256]{0:T(256)}, u32[]{:S(2)}) copy-start(f32[256]{0:T(256)} %param.22) | copy-start | bytes 3076
  102.7 18.7 %all-to-all-start.4 = ((f32[64,4,256]{2,1,0:T(4,128)}), f32[64,4,256]{2,1,0:T(4,128)S(1)}, u32[]{:S(2)}, u32[]{:S(2)}) async-start(f32[64,4,256]{2,1,0:T(4,128)} %broadcast_in_dim.128), calls=%async_computation.4 | async-start | bytes 524288 | tf_op jit(solution)/shard_map/all_to_all | solution.py:249
  108.7 14.3 %collective-permute-start.15 = (bf16[64,2374]{1,0:T(8,128)(2,1)S(1)}, bf16[64,2374]{1,0:T(8,128)(2,1)S(1)}, u32[]{:S(2)}, u32[]{:S(2)}) collective-permute-start(bf16[64,2374]{1,0:T(8,128)(2,1)S(1)} %get-tuple-element.304.r3), channel_id=1, source_target_pairs={{0,48},{16,0},{32,16},{48,32},{1,49},{17,1},{33,17},{49,33},{2,50}... | collective-permute-start | bytes 911624 | tf_op jit(solution)/shard_map/ppermute | solution.py:310
  109.9 13.1 %collective-permute-start.16 = (bf16[64,2374]{1,0:T(8,128)(2,1)S(1)}, bf16[64,2374]{1,0:T(8,128)(2,1)S(1)}, u32[]{:S(2)}, u32[]{:S(2)}) collective-permute-start(bf16[64,2374]{1,0:T(8,128)(2,1)S(1)} %get-tuple-element.304.r3), channel_id=1, source_target_pairs={{0,16},{16,32},{32,48},{48,0},{1,17},{17,33},{33,49},{49,1},{2,18}... | collective-permute-start | bytes 911624 | tf_op jit(solution)/shard_map/ppermute | solution.py:309
  123.7 9.4 %all-to-all-start.5 = ((f32[4,1,256]{2,1,0:T(1,128)}), f32[4,1,256]{2,1,0:T(1,128)S(1)}, u32[]{:S(2)}, u32[]{:S(2)}) async-start(f32[4,1,256]{2,1,0:T(1,128)} %reshape.235), calls=%async_computation.5 | async-start | bytes 8192 | tf_op jit(solution)/shard_map/all_to_all | solution.py:249
  130.3 7.0 %collective-permute-start.17 = (bf16[64,2374]{1,0:T(8,128)(2,1)S(1)}, bf16[64,2374]{1,0:T(8,128)(2,1)S(1)}, u32[]{:S(2)}, u32[]{:S(2)}) collective-permute-start(bf16[64,2374]{1,0:T(8,128)(2,1)S(1)} %broadcast_select_fusion.3), channel_id=1, source_target_pairs={{0,16},{16,32},{32,48},{48,0},{64,112},{80,64},{96,80},{112,96},{1... | collective-permute-start | bytes 911624 | tf_op jit(solution)/shard_map/ppermute | solution.py:350
  143.1 1.7 collective-permute-start.18
  145.6 21.5 %all-to-all-start.6 = ((bf16[32,40,128]{2,1,0:T(8,128)(2,1)}), bf16[32,40,128]{2,1,0:T(8,128)(2,1)S(1)}, u32[]{:S(2)}, u32[]{:S(2)}) async-start(bf16[32,40,128]{2,1,0:T(8,128)(2,1)} %bitcast.20), calls=%async_computation.6 | async-start | bytes 655360 | tf_op jit(solution)/shard_map/all_to_all | solution.py:361
  167.2 8.3 %collective-permute-start.19 = (f32[80,64]{1,0:T(8,128)S(1)}, f32[80,64]{1,0:T(8,128)S(1)}, u32[]{:S(2)}, u32[]{:S(2)}) collective-permute-start(f32[80,64]{1,0:T(8,128)S(1)} %pad_maximum_fusion.1), channel_id=1, source_target_pairs={{0,48},{16,64},{32,144},{48,224},{64,16},{80,96},{96,176},{112,192... | collective-permute-start | bytes 61448 | tf_op jit(solution)/shard_map/ppermute | solution.py:366
  175.7 0.8 copy-start
